TPU v7x, 256 devices: a whole 4x4x8 slice. The times are simulated.
256 devices in a mesh: dp: 256 (over y, z, x, core).
Axes of the slice: x: 4, y: 4, z: 8, core: 2. Of those that a mesh axis runs over, the one named last changes fastest.
Arguments:
- picture_embeddings: bfloat16 [163840, 1152], P('dp')
- caption_embeddings: bfloat16 [163840, 1152], P('dp')
- scale_exponent: float32 [1], replicated, may hold values from 2.3 to 3.4
- additive_offset: float32 [1], replicated, may hold values from -4 to -1
- opponent_round_shifts: int32 [2], replicated, may hold values from 1 to 128, as said below
Outputs:
- grad_images: bfloat16 [163840, 1152], P('dp')
- grad_texts: bfloat16 [163840, 1152], P('dp')
Inputs may be any that keep to these rules, and one draw needn't show every extreme that they name: opponent_round_shifts[0] = 128; the entries are distinct powers of two below 256, so every round pairs each block with a different partner.
All inputs are finite; a program needn't handle non-finite values.
Results may differ from a plain program's by a relative error of at most 0.0071.
Values may be sent and summed in bfloat16 or wider, within the bound.
A program may use at most 64 MiB of HBM per device.

v0:
```python
from functools import partial

import jax
import jax.numpy as jnp
from jax import lax
from jax.sharding import PartitionSpec as P

ROUNDS = 2


def for_sending(array):

    def short(part):
        return part.astype(jnp.bfloat16) if part.dtype == jnp.float32 else part

    return jax.tree.map(short, array)


def partner(array, axis, apart):
    return lax.ppermute(array, axis, [(i, i ^ 1 << apart) for i in range(lax.axis_size(axis))])


def normalize(values):
    wide = values.astype(jnp.float32)
    norms = jnp.sqrt(jnp.sum(wide * wide, axis=-1, keepdims=True) + 1e-06)
    return ((wide / norms).astype(jnp.bfloat16), norms)


def evaluate_derivatives(
    picture_embedding_group,
    caption_embedding_group,
    score_scale_factor,
    score_offset_value,
    matching_pair_indicator,
):
    similarity_score_table = (
        score_scale_factor
        * lax.dot_general(
            picture_embedding_group,
            caption_embedding_group,
            (((1,), (1,)), ((), ())),
            preferred_element_type=jnp.float32,
        )
        + score_offset_value
    )
    sig = jax.nn.sigmoid(similarity_score_table)
    if matching_pair_indicator:
        sig = sig - jnp.eye(sig.shape[0], dtype=jnp.float32)
    return sig.astype(jnp.bfloat16)


def first_operand_multiply(logistic_derivative, block):
    return lax.dot_general(
        logistic_derivative, block, (((0,), (0,)), ((), ())), preferred_element_type=jnp.float32
    )


def back_norm(values, norms, grad_unit):
    unit_wide = values.astype(jnp.float32) / norms
    inner = jnp.sum(unit_wide * grad_unit, axis=-1, keepdims=True)
    return ((grad_unit - unit_wide * inner) / norms).astype(jnp.bfloat16)


def move_text(values, bit_number):
    return jax.tree.map(
        lambda part, own: part.astype(own.dtype),
        partner(for_sending(values), "dp", bit_number),
        values,
    )


def move_grad(values, bit_number):
    return jax.tree.map(
        lambda part, own: part.astype(own.dtype),
        partner(for_sending(values), "dp", bit_number),
        values,
    )


def route(values, bit_level, mover, level_count):
    branches = [partial(mover, bit_number=number) for number in range(level_count)]
    return lax.switch(bit_level, branches, values)


def shards(
    picture_embeddings, caption_embeddings, scale_exponent, additive_offset, opponent_round_shifts
):
    score_scale_factor = jnp.exp(scale_exponent[0])
    score_offset_value = additive_offset[0]
    picture_normed_embeddings, img_norm = normalize(picture_embeddings)
    caption_normed_embeddings, txt_norm = normalize(caption_embeddings)
    level_count = lax.axis_size("dp").bit_length() - 1
    logistic_derivative = evaluate_derivatives(
        picture_normed_embeddings,
        caption_normed_embeddings,
        score_scale_factor,
        score_offset_value,
        True,
    )
    picture_embedding_derivative = score_scale_factor * jnp.dot(
        logistic_derivative, caption_normed_embeddings, preferred_element_type=jnp.float32
    )
    caption_embedding_derivative = score_scale_factor * first_operand_multiply(
        logistic_derivative, picture_normed_embeddings
    )
    for turn in range(ROUNDS):
        offset = opponent_round_shifts[turn]
        bit_level = jnp.int32(0)
        for number in range(level_count):
            bit_level = bit_level + jnp.where(offset == 1 << number, number, 0).astype(jnp.int32)
        opponent_caption_group = route(caption_normed_embeddings, bit_level, move_text, level_count)
        pairwise_similarity_scores = evaluate_derivatives(
            picture_normed_embeddings,
            opponent_caption_group,
            score_scale_factor,
            score_offset_value,
            False,
        )
        picture_embedding_derivative = picture_embedding_derivative + score_scale_factor * jnp.dot(
            pairwise_similarity_scores, opponent_caption_group, preferred_element_type=jnp.float32
        )
        objective_share = (
            score_scale_factor
            * first_operand_multiply(pairwise_similarity_scores, picture_normed_embeddings)
        ).astype(jnp.bfloat16)
        returned = route(objective_share, bit_level, move_grad, level_count)
        caption_embedding_derivative = caption_embedding_derivative + returned.astype(jnp.float32)
    grad_images = back_norm(picture_embeddings, img_norm, picture_embedding_derivative)
    grad_texts = back_norm(caption_embeddings, txt_norm, caption_embedding_derivative)
    return (grad_images, grad_texts)


def solution(mesh):
    placed = (P("dp", None), P("dp", None), P(), P(), P())
    return jax.shard_map(
        shards,
        mesh=mesh,
        in_specs=placed,
        out_specs=(P("dp", None), P("dp", None)),
        check_vma=False,
    )
```

profile of v0, /device:TPU:2, one launch (start us, length us, event | category | flops | bytes accessed | tf_op | source)
XLA Modules:
  0.0 183.1 jit_solution(5340864020946737200)
XLA Ops:
  0.6 0.0 copy-start.1
  0.7 1.9 %fusion.5 = f32[640]{0:T(1024)S(1)} fusion(bf16[640,1152]{1,0:T(8,128)(2,1)} %param.37), kind=kLoop, calls=%fused_computation.14 | loop fusion | flops 2211200 | bytes 1477120 | tf_op jit(solution)/shard_map/reduce_sum | solution.py:25
  3.2 1.7 fusion.6
  5.0 1.1 fusion.7
  6.1 0.0 copy-start.6
  6.1 0.0 copy-start.8
  6.8 1.5 subtract_convert_fusion
  8.3 0.0 copy-start.10
  8.3 3.0 %fusion.10 = f32[640,1152]{1,0:T(8,128)} fusion(bf16[640,640]{1,0:T(8,128)(2,1)S(1)} %subtract_convert_fusion, bf16[640,1152]{1,0:T(8,128)(2,1)S(1)} %get-tuple-element.89), kind=kOutput, calls=%fused_computation.29 | convolution fusion | flops 943718400 | bytes 5242880 | tf_op jit(solution)/shard_map/dot_general | solution.py:100
  11.3 0.6 fusion.9
  16.7 35.7 %conditional.10 = (bf16[640,1152]{1,0:T(8,128)(2,1)}) conditional(s32[]{:T(128)} %bitcast.2, bf16[640,1152]{1,0:T(8,128)(2,1)S(1)} %get-tuple-element.89, bf16[640,1152]{1,0:T(8,128)(2,1)S(1)} %get-tuple-element.89, bf16[640,1152]{1,0:T(8,128)(2,1)S(1)} %get-tuple-element.89, ...), branch_computations={%region_2.3_spmd, %region_3.4_spmd, %region_4.5_spmd, %region_5.6_... | conditional | bytes 5898288 | solution.py:82
  16.7 3.3 %collective-permute-start.7 = (bf16[640,1152]{1,0:T(8,128)(2,1)S(1)}, bf16[640,1152]{1,0:T(8,128)(2,1)}, u32[]{:S(2)}, u32[]{:S(2)}) collective-permute-start(bf16[640,1152]{1,0:T(8,128)(2,1)S(1)} %param.7), channel_id=1, source_target_pairs={{0,128},{1,129},{2,130},{3,131},{4,132},{5,133},{6,134},{7,135},{8... | collective-permute-start | bytes 4423688 | tf_op jit(solution)/shard_map/cond/branch_7_fun/ppermute | solution.py:20
  20.0 32.4 %collective-permute-done.7 = bf16[640,1152]{1,0:T(8,128)(2,1)} collective-permute-done((bf16[640,1152]{1,0:T(8,128)(2,1)S(1)}, bf16[640,1152]{1,0:T(8,128)(2,1)}, u32[]{:S(2)}, u32[]{:S(2)}) %collective-permute-start.7) | collective-permute-done | bytes 1474592 | tf_op jit(solution)/shard_map/cond/branch_7_fun/ppermute | solution.py:20
  52.4 3.4 %divide_convert_fusion.3 = bf16[640,640]{1,0:T(8,128)(2,1)S(1)} fusion(bf16[640,1152]{1,0:T(8,128)(2,1)} %copy-done.6, bf16[640,1152]{1,0:T(8,128)(2,1)} %get-tuple-element.90, f32[]{:T(128)} %bitcast.24, f32[]{:T(128)} %bitcast), kind=kOutput, calls=%fused_computation.21 | convolution fusion | flops 946176000 | bytes 3768328 | tf_op jit(solution)/shard_map/dot_general | solution.py:38
  55.9 0.0 copy-start.9
  55.9 4.7 %convolution_add_fusion.1 = f32[640,1152]{1,0:T(8,128)} fusion(f32[640,1152]{1,0:T(8,128)S(1)} %copy-done.3, bf16[640,640]{1,0:T(8,128)(2,1)S(1)} %divide_convert_fusion.3, bf16[640,1152]{1,0:T(8,128)(2,1)} %get-tuple-element.90), kind=kOutput, calls=%fused_computation.6 | convolution fusion | flops 944455680 | bytes 8192000 | tf_op jit(solution)/shard_map/dot_general | solution.py:119
  64.9 33.6 %conditional.11 = (bf16[640,1152]{1,0:T(8,128)(2,1)}) conditional(s32[]{:T(128)} %bitcast.3, bf16[640,1152]{1,0:T(8,128)(2,1)S(1)} %copy-done.9, bf16[640,1152]{1,0:T(8,128)(2,1)S(1)} %copy-done.9, bf16[640,1152]{1,0:T(8,128)(2,1)S(1)} %copy-done.9, bf16[640,1152]{1,0:T(8,128)(2,1)S(1)} %copy-done.9, ...), branch_computations={%region_10.11_spmd, %region_11.12_spmd, %region_12.13_spmd, %regio... | conditional | bytes 5898288 | solution.py:82
  64.9 2.0 %collective-permute-start.11 = (bf16[640,1152]{1,0:T(8,128)(2,1)S(1)}, bf16[640,1152]{1,0:T(8,128)(2,1)}, u32[]{:S(2)}, u32[]{:S(2)}) collective-permute-start(bf16[640,1152]{1,0:T(8,128)(2,1)S(1)} %param.11), channel_id=1, source_target_pairs={{0,8},{1,9},{2,10},{3,11},{4,12},{5,13},{6,14},{7,15},{8,0},{9,1},... | collective-permute-start | bytes 4423688 | tf_op jit(solution)/shard_map/cond/branch_3_fun/ppermute | solution.py:20
  66.9 31.5 %collective-permute-done.11 = bf16[640,1152]{1,0:T(8,128)(2,1)} collective-permute-done((bf16[640,1152]{1,0:T(8,128)(2,1)S(1)}, bf16[640,1152]{1,0:T(8,128)(2,1)}, u32[]{:S(2)}, u32[]{:S(2)}) %collective-permute-start.11) | collective-permute-done | bytes 1474592 | tf_op jit(solution)/shard_map/cond/branch_3_fun/ppermute | solution.py:20
  98.5 3.4 %divide_convert_fusion.2 = bf16[640,640]{1,0:T(8,128)(2,1)S(1)} fusion(bf16[640,1152]{1,0:T(8,128)(2,1)} %copy-done.6, bf16[640,1152]{1,0:T(8,128)(2,1)} %get-tuple-element.91, f32[]{:T(128)} %bitcast.23, f32[]{:T(128)} %bitcast), kind=kOutput, calls=%fused_computation.20 | convolution fusion | flops 946176000 | bytes 3768328 | tf_op jit(solution)/shard_map/dot_general | solution.py:38
  101.9 3.0 %multiply_reduce_fusion.1 = (f32[640]{0:T(1024)S(1)}, f32[640,1152]{1,0:T(8,128)S(1)}) fusion(f32[640]{0:T(1024)S(1)} %add_sqrt_fusion.1, bf16[640,1152]{1,0:T(8,128)(2,1)S(1)} %copy-done, f32[]{:T(128)} %bitcast, f32[640,1152]{1,0:T(8,128)S(1)} %copy-done.2, bf16[640,640]{1,0:T(8,128)(2,1)S(1)} %divide_convert_fusion.2, ...), kind=kOutput, calls=%fused_computation.19 | convolution fusion | flops 948141440 | bytes 9671684 | tf_op jit(solution)/shard_map/dot_general | solution.py:119
  104.9 1.8 divide_convert_fusion.1
  106.7 1.4 fusion.4
  108.1 32.6 %conditional.13 = (bf16[640,1152]{1,0:T(8,128)(2,1)}) conditional(s32[]{:T(128)} %bitcast.3, bf16[640,1152]{1,0:T(8,128)(2,1)S(1)} %fusion.4, bf16[640,1152]{1,0:T(8,128)(2,1)S(1)} %fusion.4, bf16[640,1152]{1,0:T(8,128)(2,1)S(1)} %fusion.4, bf16[640,1152]{1,0:T(8,128)(2,1)S(1)} %fusion.4, ...), branch_computations={%region_27.28_spmd, %region_28.29_spmd, %region_29.30_spmd, %regio... | conditional | bytes 5898288
  108.2 1.8 %collective-permute-start.27 = (bf16[640,1152]{1,0:T(8,128)(2,1)S(1)}, bf16[640,1152]{1,0:T(8,128)(2,1)}, u32[]{:S(2)}, u32[]{:S(2)}) collective-permute-start(bf16[640,1152]{1,0:T(8,128)(2,1)S(1)} %param.27), channel_id=1, source_target_pairs={{0,8},{1,9},{2,10},{3,11},{4,12},{5,13},{6,14},{7,15},{8,0},{9,1},... | collective-permute-start | bytes 4423688 | tf_op jit(solution)/shard_map/cond/branch_3_fun/ppermute | solution.py:20
  110.0 30.8 %collective-permute-done.27 = bf16[640,1152]{1,0:T(8,128)(2,1)} collective-permute-done((bf16[640,1152]{1,0:T(8,128)(2,1)S(1)}, bf16[640,1152]{1,0:T(8,128)(2,1)}, u32[]{:S(2)}, u32[]{:S(2)}) %collective-permute-start.27) | collective-permute-done | bytes 1474592 | tf_op jit(solution)/shard_map/cond/branch_3_fun/ppermute | solution.py:20
  140.8 2.9 %fusion.3 = bf16[640,1152]{1,0:T(8,128)(2,1)S(1)} fusion(bf16[640,640]{1,0:T(8,128)(2,1)S(1)} %copy-done.5, bf16[640,1152]{1,0:T(8,128)(2,1)} %copy-done.6, f32[]{:T(128)} %bitcast), kind=kOutput, calls=%fused_computation.12 | convolution fusion | flops 945192960 | bytes 3768324 | tf_op jit(solution)/shard_map/dot_general | solution.py:53
  143.7 33.2 %conditional.12 = (bf16[640,1152]{1,0:T(8,128)(2,1)}) conditional(s32[]{:T(128)} %bitcast.2, bf16[640,1152]{1,0:T(8,128)(2,1)S(1)} %fusion.3, bf16[640,1152]{1,0:T(8,128)(2,1)S(1)} %fusion.3, bf16[640,1152]{1,0:T(8,128)(2,1)S(1)} %fusion.3, bf16[640,1152]{1,0:T(8,128)(2,1)S(1)} %fusion.3, ...), branch_computations={%region_19.20_spmd, %region_20.21_spmd, %region_21.22_spmd, %regio... | conditional | bytes 5898288
  143.7 3.3 %collective-permute-start.23 = (bf16[640,1152]{1,0:T(8,128)(2,1)S(1)}, bf16[640,1152]{1,0:T(8,128)(2,1)}, u32[]{:S(2)}, u32[]{:S(2)}) collective-permute-start(bf16[640,1152]{1,0:T(8,128)(2,1)S(1)} %param.23), channel_id=1, source_target_pairs={{0,128},{1,129},{2,130},{3,131},{4,132},{5,133},{6,134},{7,135},{8... | collective-permute-start | bytes 4423688 | tf_op jit(solution)/shard_map/cond/branch_7_fun/ppermute | solution.py:20
  147.0 29.9 %collective-permute-done.23 = bf16[640,1152]{1,0:T(8,128)(2,1)} collective-permute-done((bf16[640,1152]{1,0:T(8,128)(2,1)S(1)}, bf16[640,1152]{1,0:T(8,128)(2,1)}, u32[]{:S(2)}, u32[]{:S(2)}) %collective-permute-start.23) | collective-permute-done | bytes 1474592 | tf_op jit(solution)/shard_map/cond/branch_7_fun/ppermute | solution.py:20
  176.9 4.4 %multiply_reduce_fusion = (f32[640]{0:T(1024)S(1)}, f32[640,1152]{1,0:T(8,128)S(1)}) fusion(f32[640]{0:T(1024)S(1)} %add_sqrt_fusion, bf16[640,1152]{1,0:T(8,128)(2,1)S(1)} %copy-done.1, bf16[640,1152]{1,0:T(8,128)(2,1)} %get-tuple-element.93, bf16[640,1152]{1,0:T(8,128)(2,1)} %get-tuple-element.92, bf16[640,640]{1,0:T(8,128)(2,1)S(1)} %copy-done.12, ...), kind=kOutput, calls=%fused_computation.17 | convolution fusion | flops 950353280 | bytes 9671684 | tf_op jit(solution)/shard_map/dot_general | solution.py:53
  181.4 1.8 divide_convert_fusion
  (23 shorter events, 0.1 us)
Async XLA Ops:
  0.6 4.4 %copy-start = (bf16[640,1152]{1,0:T(8,128)(2,1)S(1)}, bf16[640,1152]{1,0:T(8,128)(2,1)}, u32[]{:S(2)}) copy-start(bf16[640,1152]{1,0:T(8,128)(2,1)} %param.37) | copy-start | bytes 4423684
  0.6 4.4 %copy-start.1 = (bf16[640,1152]{1,0:T(8,128)(2,1)S(1)}, bf16[640,1152]{1,0:T(8,128)(2,1)}, u32[]{:S(2)}) copy-start(bf16[640,1152]{1,0:T(8,128)(2,1)} %param.38) | copy-start | bytes 4423684
  6.1 2.2 %copy-start.6 = (bf16[640,1152]{1,0:T(8,128)(2,1)}, bf16[640,1152]{1,0:T(8,128)(2,1)S(1)}, u32[]{:S(2)}) copy-start(bf16[640,1152]{1,0:T(8,128)(2,1)S(1)} %get-tuple-element.88) | copy-start | bytes 4423684
  6.1 10.5 %copy-start.8 = (bf16[640,1152]{1,0:T(8,128)(2,1)}, bf16[640,1152]{1,0:T(8,128)(2,1)S(1)}, u32[]{:S(2)}) copy-start(bf16[640,1152]{1,0:T(8,128)(2,1)S(1)} %get-tuple-element.89) | copy-start | bytes 4423684
  8.3 3.0 %copy-start.11 = (bf16[640,640]{1,0:T(8,128)(2,1)}, bf16[640,640]{1,0:T(8,128)(2,1)S(1)}, u32[]{:S(2)}) copy-start(bf16[640,640]{1,0:T(8,128)(2,1)S(1)} %subtract_convert_fusion) | copy-start | bytes 2457604
  8.3 3.0 %copy-start.10 = (s32[2]{0:T(128)S(1)}, s32[2]{0:T(128)}, u32[]{:S(2)}) copy-start(s32[2]{0:T(128)} %param.41) | copy-start | bytes 28
  16.7 35.7 %collective-permute-start.7 = (bf16[640,1152]{1,0:T(8,128)(2,1)S(1)}, bf16[640,1152]{1,0:T(8,128)(2,1)}, u32[]{:S(2)}, u32[]{:S(2)}) collective-permute-start(bf16[640,1152]{1,0:T(8,128)(2,1)S(1)} %param.7), channel_id=1, source_target_pairs={{0,128},{1,129},{2,130},{3,131},{4,132},{5,133},{6,134},{7,135},{8... | collective-permute-start | bytes 4423688 | tf_op jit(solution)/shard_map/cond/branch_7_fun/ppermute | solution.py:20
  52.4 3.4 %copy-start.3 = (f32[640,1152]{1,0:T(8,128)S(1)}, f32[640,1152]{1,0:T(8,128)}, u32[]{:S(2)}) copy-start(f32[640,1152]{1,0:T(8,128)} %fusion.10) | copy-start | bytes 8847364
  55.8 4.7 %copy-start.4 = (bf16[640,640]{1,0:T(8,128)(2,1)}, bf16[640,640]{1,0:T(8,128)(2,1)S(1)}, u32[]{:S(2)}) copy-start(bf16[640,640]{1,0:T(8,128)(2,1)S(1)} %divide_convert_fusion.3) | copy-start | bytes 2457604
  55.9 9.0 %copy-start.9 = (bf16[640,1152]{1,0:T(8,128)(2,1)S(1)}, bf16[640,1152]{1,0:T(8,128)(2,1)}, u32[]{:S(2)}) copy-start(bf16[640,1152]{1,0:T(8,128)(2,1)} %copy-done.8) | copy-start | bytes 4423684
  64.9 33.5 %collective-permute-start.11 = (bf16[640,1152]{1,0:T(8,128)(2,1)S(1)}, bf16[640,1152]{1,0:T(8,128)(2,1)}, u32[]{:S(2)}, u32[]{:S(2)}) collective-permute-start(bf16[640,1152]{1,0:T(8,128)(2,1)S(1)} %param.11), channel_id=1, source_target_pairs={{0,8},{1,9},{2,10},{3,11},{4,12},{5,13},{6,14},{7,15},{8,0},{9,1},... | collective-permute-start | bytes 4423688 | tf_op jit(solution)/shard_map/cond/branch_3_fun/ppermute | solution.py:20
  98.5 3.4 %copy-start.2 = (f32[640,1152]{1,0:T(8,128)S(1)}, f32[640,1152]{1,0:T(8,128)}, u32[]{:S(2)}) copy-start(f32[640,1152]{1,0:T(8,128)} %convolution_add_fusion.1) | copy-start | bytes 8847364
  104.9 1.8 copy-start.7
  106.7 34.1 %copy-start.5 = (bf16[640,640]{1,0:T(8,128)(2,1)S(1)}, bf16[640,640]{1,0:T(8,128)(2,1)}, u32[]{:S(2)}) copy-start(bf16[640,640]{1,0:T(8,128)(2,1)} %copy-done.4) | copy-start | bytes 2457604
  108.2 32.6 %collective-permute-start.27 = (bf16[640,1152]{1,0:T(8,128)(2,1)S(1)}, bf16[640,1152]{1,0:T(8,128)(2,1)}, u32[]{:S(2)}, u32[]{:S(2)}) collective-permute-start(bf16[640,1152]{1,0:T(8,128)(2,1)S(1)} %param.27), channel_id=1, source_target_pairs={{0,8},{1,9},{2,10},{3,11},{4,12},{5,13},{6,14},{7,15},{8,0},{9,1},... | collective-permute-start | bytes 4423688 | tf_op jit(solution)/shard_map/cond/branch_3_fun/ppermute | solution.py:20
  140.8 36.1 %copy-start.12 = (bf16[640,640]{1,0:T(8,128)(2,1)S(1)}, bf16[640,640]{1,0:T(8,128)(2,1)}, u32[]{:S(2)}) copy-start(bf16[640,640]{1,0:T(8,128)(2,1)} %copy-done.11) | copy-start | bytes 2457604
  143.7 33.2 %collective-permute-start.23 = (bf16[640,1152]{1,0:T(8,128)(2,1)S(1)}, bf16[640,1152]{1,0:T(8,128)(2,1)}, u32[]{:S(2)}, u32[]{:S(2)}) collective-permute-start(bf16[640,1152]{1,0:T(8,128)(2,1)S(1)} %param.23), channel_id=1, source_target_pairs={{0,128},{1,129},{2,130},{3,131},{4,132},{5,133},{6,134},{7,135},{8... | collective-permute-start | bytes 4423688 | tf_op jit(solution)/shard_map/cond/branch_7_fun/ppermute | solution.py:20
where the time goes:
time: 184 us; the launch traced here: 183 us
  waiting for transfers between devices  125 us (68%)
  matrix products  27.8 us (15%)
  between operations  11.3 us (6%)
  starting transfers between devices  10.4 us (6%)
  other arithmetic  8.24 us (4%)
    ppermute x4, waiting for transfers between devices, partner(): lax.ppermute(array, axis, [(i, i ^ 1 << apart) for i in range(lax.axis_si...  125 us
    ppermute x4, starting transfers between devices, partner(): lax.ppermute(array, axis, [(i, i ^ 1 << apart) for i in range(lax.axis_si...  10.4 us
    dot_general x3, matrix products, first_operand_multiply(): lax.dot_general(logistic_derivative, block, (((0,), (0,)), ((), ())), pre...  8.77 us
    dot_general x3, matrix products, evaluate_derivatives(): lax.dot_general(picture_embedding_group, caption_embedding_group, (((1,),...  8.31 us
    dot_general x2, matrix products, shards(): jnp.dot(pairwise_similarity_scores, opponent_caption_group, preferred_ele...  7.69 us
  transfers between devices with their start and end apart: 4, of which 4 were waited for; matrix products, arithmetic and copies ran while one was open for 0% of the time, Pallas kernels for 0%

commit v1 on v0

v1 whole, which is shorter than its diff:
```python
import functools

import jax
import jax.numpy as jnp
from jax import lax
from jax.experimental import pallas as pl
from jax.experimental.pallas import tpu as pltpu
from jax.sharding import PartitionSpec as P

MESH = pl.DeviceIdType.MESH
CHUNK = 64
TILE = 128


def rows_at(index, size):
    return pl.ds(pl.multiple_of(index * size, size), size)


def dot_nt(a, b):
    return lax.dot_general(a, b, (((1,), (1,)), ((), ())), preferred_element_type=jnp.float32)


def dot_tn(a, b):
    return lax.dot_general(a, b, (((0,), (0,)), ((), ())), preferred_element_type=jnp.float32)


def dot_nn(a, b):
    return jnp.dot(a, b, preferred_element_type=jnp.float32)


def inverse_norm(wide):
    return 1.0 / jnp.sqrt(jnp.sum(wide * wide, axis=-1, keepdims=True) + 1e-06)


def back_norm(raw, inverse, grad_unit):
    unit = raw.astype(jnp.float32) * inverse
    inner = jnp.sum(unit * grad_unit, axis=-1, keepdims=True)
    return ((grad_unit - unit * inner) * inverse).astype(jnp.bfloat16)


def kernel(
    n,
    shift,
    scale_ref,
    offset_ref,
    img_in,
    txt_in,
    img_out,
    txt_out,
    img_raw,
    txt_raw,
    img_unit,
    txt_unit,
    img_inv,
    txt_inv,
    held,
    slopes,
    txt_grad,
    part,
    returned,
    img_res,
    txt_res,
    img_load,
    txt_load,
    img_store,
    txt_store,
    text_send,
    text_recv,
    part_send,
    part_recv,
):
    rows = img_in.shape[0]
    chunks, tiles = rows // CHUNK, rows // TILE
    me = lax.axis_index("dp")
    across = me ^ (n // 2)
    near = me ^ shift
    far = me ^ (n // 2) ^ shift
    relayed = shift == n // 4
    first, second = (far, near) if relayed else (across, near)

    def load_text(c):
        at = rows_at(c, CHUNK)
        return pltpu.make_async_copy(txt_in.at[at], txt_raw.at[at], txt_load.at[c])

    def load_image(i):
        at = rows_at(i, TILE)
        return pltpu.make_async_copy(img_in.at[at], img_raw.at[at], img_load.at[i])

    def store_text(c):
        at = rows_at(c, CHUNK)
        return pltpu.make_async_copy(txt_res.at[at], txt_out.at[at], txt_store.at[c])

    def store_image(i):
        at = rows_at(i, TILE)
        return pltpu.make_async_copy(img_res.at[at], img_out.at[at], img_store.at[i])

    def send_text(r, c, source, device):
        at = rows_at(c, CHUNK)
        return pltpu.make_async_remote_copy(
            src_ref=source.at[at],
            dst_ref=held.at[r, at],
            send_sem=text_send.at[r, c],
            recv_sem=text_recv.at[r, c],
            device_id=(device,),
            device_id_type=MESH,
        )

    def send_part(r, c, device):
        at = rows_at(c, CHUNK)
        return pltpu.make_async_remote_copy(
            src_ref=part.at[r, at],
            dst_ref=returned.at[r, at],
            send_sem=part_send.at[r, c],
            recv_sem=part_recv.at[r, c],
            device_id=(device,),
            device_id_type=MESH,
        )

    @pl.loop(0, chunks)
    def _(c):
        load_text(c).start()

    @pl.loop(0, tiles)
    def _(i):
        load_image(i).start()

    barrier = pltpu.get_barrier_semaphore()
    for device in (first, second):
        pl.semaphore_signal(barrier, inc=1, device_id=(device,), device_id_type=MESH)
    pl.semaphore_wait(barrier, 2)

    scale = jnp.exp(jnp.full((1, 1), scale_ref[0], jnp.float32))
    offset = offset_ref[0]

    @pl.loop(0, chunks)
    def _(c):
        at = rows_at(c, CHUNK)
        load_text(c).wait()
        wide = txt_raw[at, :].astype(jnp.float32)
        inverse = inverse_norm(wide)
        txt_inv[at, :] = inverse
        txt_unit[at, :] = (wide * inverse).astype(jnp.bfloat16)
        if not relayed:
            send_text(0, c, txt_unit, first).start()
        send_text(1, c, txt_unit, second).start()

    @pl.loop(0, tiles)
    def _(i):
        at = rows_at(i, TILE)
        load_image(i).wait()
        wide = img_raw[at, :].astype(jnp.float32)
        inverse = inverse_norm(wide)
        img_inv[at, :] = inverse
        img_unit[at, :] = (wide * inverse).astype(jnp.bfloat16)

    @pl.loop(0, tiles)
    def _(i):
        at = rows_at(i, TILE)
        logits = dot_nt(txt_unit[at, :], img_unit[...]) * scale + offset
        slope = 1.0 / (1.0 + jnp.exp(-logits))
        row = lax.broadcasted_iota(jnp.int32, slope.shape, 0) + i * TILE
        column = lax.broadcasted_iota(jnp.int32, slope.shape, 1)
        slope = jnp.where(row == column, slope - 1.0, slope).astype(jnp.bfloat16)
        slopes[0, at, :] = slope
        txt_grad[at, :] = scale * dot_nn(slope, img_unit[...])

    def respond(r, c):
        at = rows_at(c, CHUNK)
        logits = dot_nt(held[r, at, :], img_unit[...]) * scale + offset
        slope = (1.0 / (1.0 + jnp.exp(-logits))).astype(jnp.bfloat16)
        slopes[r + 1, at, :] = slope
        part[r, at, :] = (scale * dot_nn(slope, img_unit[...])).astype(jnp.bfloat16)

    if relayed:

        @pl.loop(0, chunks + 2)
        def _(step):
            @pl.when(step < chunks)
            def _():
                send_text(1, step, txt_unit, second).wait_recv()
                send_text(0, step, held.at[1], first).start()
                respond(1, step)

            @pl.when((step >= 1) & (step < chunks + 1))
            def _():
                c = step - 1
                send_text(0, c, held.at[1], first).wait_recv()
                respond(0, c)
                send_part(0, c, first).start()

            @pl.when(step >= 2)
            def _():
                c = step - 2
                at = rows_at(c, CHUNK)
                send_part(0, c, first).wait_recv()
                total = part[1, at, :].astype(jnp.float32) + returned[0, at, :].astype(jnp.float32)
                part[1, at, :] = total.astype(jnp.bfloat16)
                send_part(1, c, second).start()

    else:

        @pl.loop(0, chunks)
        def _(c):
            for r, device in ((1, second), (0, first)):
                send_text(r, c, txt_unit, device).wait_recv()
                respond(r, c)
                send_part(r, c, device).start()

    @pl.loop(0, tiles)
    def _(i):
        at = rows_at(i, TILE)
        grad = dot_tn(slopes[0, :, at], txt_unit[...])
        grad += dot_tn(slopes[1, :, at], held[0])
        grad += dot_tn(slopes[2, :, at], held[1])
        img_res[at, :] = back_norm(img_raw[at, :], img_inv[at, :], scale * grad)
        store_image(i).start()

    @pl.loop(0, chunks)
    def _(c):
        at = rows_at(c, CHUNK)
        grad = txt_grad[at, :]
        send_part(1, c, second).wait_recv()
        grad += returned[1, at, :].astype(jnp.float32)
        if not relayed:
            send_part(0, c, first).wait_recv()
            grad += returned[0, at, :].astype(jnp.float32)
        txt_res[at, :] = back_norm(txt_raw[at, :], txt_inv[at, :], grad)
        store_text(c).start()

    @pl.loop(0, chunks)
    def _(c):
        for r, device in ((0, first), (1, second)):
            send_text(r, c, txt_unit, device).wait_send()
            send_part(r, c, device).wait_send()
        store_text(c).wait()

    @pl.loop(0, tiles)
    def _(i):
        store_image(i).wait()


def exchange(n, level, img, txt, scale_exponent, additive_offset):
    rows, width = img.shape
    chunks, tiles = rows // CHUNK, rows // TILE
    block = functools.partial(pltpu.VMEM, (rows, width))
    pair = functools.partial(pltpu.VMEM, (2, rows, width))
    return pl.pallas_call(
        functools.partial(kernel, n, 1 << level),
        out_shape=(
            jax.ShapeDtypeStruct((rows, width), jnp.bfloat16),
            jax.ShapeDtypeStruct((rows, width), jnp.bfloat16),
        ),
        in_specs=[pl.BlockSpec(memory_space=pltpu.SMEM)] * 2
        + [pl.BlockSpec(memory_space=pl.ANY)] * 2,
        out_specs=[pl.BlockSpec(memory_space=pl.ANY)] * 2,
        scratch_shapes=[
            block(jnp.bfloat16),
            block(jnp.bfloat16),
            block(jnp.bfloat16),
            block(jnp.bfloat16),
            pltpu.VMEM((rows, 1), jnp.float32),
            pltpu.VMEM((rows, 1), jnp.float32),
            pair(jnp.bfloat16),
            pltpu.VMEM((3, rows, rows), jnp.bfloat16),
            block(jnp.float32),
            pair(jnp.bfloat16),
            pair(jnp.bfloat16),
            block(jnp.bfloat16),
            block(jnp.bfloat16),
            pltpu.SemaphoreType.DMA((tiles,)),
            pltpu.SemaphoreType.DMA((chunks,)),
            pltpu.SemaphoreType.DMA((tiles,)),
            pltpu.SemaphoreType.DMA((chunks,)),
            pltpu.SemaphoreType.DMA((2, chunks)),
            pltpu.SemaphoreType.DMA((2, chunks)),
            pltpu.SemaphoreType.DMA((2, chunks)),
            pltpu.SemaphoreType.DMA((2, chunks)),
        ],
        compiler_params=pltpu.CompilerParams(
            collective_id=level, has_side_effects=True, vmem_limit_bytes=40 * 2**20
        ),
        name=f"exchange_{level}",
    )(scale_exponent, additive_offset, img, txt)


def solution(mesh):
    n = mesh.shape["dp"]
    levels = n.bit_length() - 2

    def step(img, txt, scale_exponent, additive_offset, shifts):
        level = 31 - lax.clz(shifts[1])
        branches = [functools.partial(exchange, n, k) for k in range(levels)]
        return lax.switch(level, branches, img, txt, scale_exponent, additive_offset)

    placed = (P("dp", None), P("dp", None), P(), P(), P())
    return jax.shard_map(
        step,
        mesh=mesh,
        in_specs=placed,
        out_specs=(P("dp", None), P("dp", None)),
        check_vma=False,
    )
```

time: 184 us -> 78.2 us (0.42)
  waiting for transfers between devices: 125 us -> 0 us
  Pallas kernels: 0 us -> 72.1 us
  matrix products: 27.8 us -> 0 us
  starting transfers between devices: 10.4 us -> 0 us
  between operations: 11.3 us -> 1.29 us
  other arithmetic: 8.24 us -> 0 us
  local copies, waits for them, and re-layouts: 0.66 us -> 3.46 us
    ppermute x4 -> x0, waiting for transfers between devices: 125 us -> none  [partner(): lax.ppermute(array, axis, [(i, i ^ 1 << apart) for i in range(lax.axis_si...]
    pallas_call x0 -> x1, Pallas kernels: none -> 72.1 us  [exchange(): pl.pallas_call(functools.partial(kernel, n, 1 << level), out_shape=(jax.S...]
    dot_general x9 -> x0, matrix products: 27.8 us -> none  [the longest x3 8.77 us: first_operand_multiply(): lax.dot_general(logistic_derivative, block, (((0,), (0,)), ((), ())), pre...]
    ppermute x4 -> x0, starting transfers between devices: 10.4 us -> none  [partner(): lax.ppermute(array, axis, [(i, i ^ 1 << apart) for i in range(lax.axis_si...]
    convert_element_type x3 -> x0, other arithmetic: 4.61 us -> none  [the longest x2 3.52 us: back_norm(): return ((grad_unit - unit_wide * inner) / norms).astype(jnp.bfloat16)]
    reduce_sum x2 -> x0, other arithmetic: 3.62 us -> none  [normalize(): norms = jnp.sqrt(jnp.sum(wide * wide, axis=-1, keepdims=True) + 1e-06)]
    unnamed x26 -> x2, local copies, waits for them, and re-layouts: 0.06 us -> 2.22 us
  transfers between devices with their start and end apart: 4 -> 0, of which waited for: 4 -> 0; matrix products, arithmetic and copies ran while one was open for 0% -> 0% of each run, Pallas kernels for 0% -> 0%
where the time goes in v1:
time: 78.2 us; the launch traced here: 77.1 us
  Pallas kernels  72.1 us (92%)
  local copies, waits for them, and re-layouts  3.46 us (4%)
  between operations  1.29 us (2%)
    pallas_call x1, Pallas kernels, exchange(): pl.pallas_call(functools.partial(kernel, n, 1 << level), out_shape=(jax.S...  72.1 us
    unnamed x2, local copies, waits for them, and re-layouts  2.22 us

profile of v1, /device:TPU:2, one launch (start us, length us, event | category | flops | bytes accessed | tf_op | source)
XLA Modules:
  0.0 77.1 jit_solution(10381089432664335779)
XLA Ops:
  0.6 1.2 %slice.3 = s32[1]{0:T(128)} slice(s32[2]{0:T(128)} %param.16), slice={[1:2]} | slice | bytes 8 | tf_op jit(solution)/shard_map/slice | solution.py:291
  2.5 72.4 %conditional.1 = ((bf16[640,1152]{1,0:T(8,128)(2,1)S(1)}, bf16[640,1152]{1,0:T(8,128)(2,1)S(1)})) conditional(s32[]{:T(128)} %bitcast, (f32[1]{0:T(128)}, f32[1]{0:T(128)}, bf16[640,1152]{1,0:T(8,128)(2,1)}, bf16[640,1152]{1,0:T(8,128)(2,1)}) %tuple.28, (f32[1]{0:T(128)}, f32[1]{0:T(128)}, ...), branch_computations={%region_0.0_spmd, %region_1.0_spmd, %region_2.0_spmd, %region_3.0_... | conditional | bytes 8 | solution.py:293
  2.6 72.1 %exchange_2.1 = (bf16[640,1152]{1,0:T(8,128)(2,1)S(1)}, bf16[640,1152]{1,0:T(8,128)(2,1)S(1)}) custom-call(f32[1]{0:T(128)} %get-tuple-element.64.scale_ref, f32[1]{0:T(128)} %get-tuple-element.65.offset_ref, bf16[640,1152]{1,0:T(8,128)(2,1)} %get-tuple-element.66.img_in, bf16[640,1152]{1,0:T(8,128)(2,1)} %get-tuple-element.67.txt_in), custom_call_target="tpu_custom_call" | custom-call | tf_op jit(solution)/shard_map/cond/branch_2_fun/exchange_2/pallas_call | solution.py:247
  74.9 1.1 %copy.37 = bf16[640,1152]{1,0:T(8,128)(2,1)} copy(bf16[640,1152]{1,0:T(8,128)(2,1)S(1)} %get-tuple-element.118) | data formatting | bytes 2949120
  76.0 1.1 %copy.38 = bf16[640,1152]{1,0:T(8,128)(2,1)} copy(bf16[640,1152]{1,0:T(8,128)(2,1)S(1)} %get-tuple-element.119) | data formatting | bytes 2949120

commit v2 on v1

v2 whole, which is shorter than its diff:
```python
import functools

import jax
import jax.numpy as jnp
from jax import lax
from jax.experimental import pallas as pl
from jax.experimental.pallas import tpu as pltpu
from jax.sharding import PartitionSpec as P

MESH = pl.DeviceIdType.MESH
TILE = 128
AHEAD = 2
LAG = 2


def rows_at(index, size):
    return pl.ds(pl.multiple_of(index * size, size), size)


def dot_nt(a, b):
    return lax.dot_general(a, b, (((1,), (1,)), ((), ())), preferred_element_type=jnp.float32)


def dot_tn(a, b):
    return lax.dot_general(a, b, (((0,), (0,)), ((), ())), preferred_element_type=jnp.float32)


def dot_nn(a, b):
    return jnp.dot(a, b, preferred_element_type=jnp.float32)


def phase(name, count):
    def run(body):
        with jax.named_scope(name):
            pl.loop(0, count)(body)

    return run


def inverse_norm(wide):
    return 1.0 / jnp.sqrt(jnp.sum(wide * wide, axis=-1, keepdims=True) + 1e-06)


def back_norm(raw, inverse, grad_unit):
    unit = raw.astype(jnp.float32) * inverse
    inner = jnp.sum(unit * grad_unit, axis=-1, keepdims=True)
    return ((grad_unit - unit * inner) * inverse).astype(jnp.bfloat16)


def kernel(
    n,
    shift,
    chunk,
    scale_ref,
    offset_ref,
    img_in,
    txt_in,
    img_out,
    txt_out,
    img_raw,
    txt_raw,
    img_unit,
    txt_unit,
    img_inv,
    txt_inv,
    held,
    slopes,
    txt_grad,
    part,
    returned,
    img_load,
    txt_load,
    text_send,
    text_recv,
    part_send,
    part_recv,
):
    rows = img_in.shape[0]
    chunks, tiles = rows // chunk, rows // TILE
    per = chunks // tiles
    me = lax.axis_index("dp")
    across = me ^ (n // 2)
    near = me ^ shift
    far = me ^ (n // 2) ^ shift
    relayed = shift == n // 4
    first, second = (far, near) if relayed else (across, near)

    def load_text(c):
        at = rows_at(c, chunk)
        return pltpu.make_async_copy(txt_in.at[at], txt_raw.at[at], txt_load.at[c])

    def load_image(i):
        at = rows_at(i, TILE)
        return pltpu.make_async_copy(img_in.at[at], img_raw.at[at], img_load.at[i])

    def send_text(r, c, source, device):
        at = rows_at(c, chunk)
        return pltpu.make_async_remote_copy(
            src_ref=source.at[at],
            dst_ref=held.at[r, at],
            send_sem=text_send.at[r, c],
            recv_sem=text_recv.at[r, c],
            device_id=(device,),
            device_id_type=MESH,
        )

    def send_part(r, c, device):
        at = rows_at(c, chunk)
        return pltpu.make_async_remote_copy(
            src_ref=part.at[r, at],
            dst_ref=returned.at[r, at],
            send_sem=part_send.at[r, c],
            recv_sem=part_recv.at[r, c],
            device_id=(device,),
            device_id_type=MESH,
        )

    @phase("load_text", chunks)
    def _(c):
        load_text(c).start()

    @phase("load_image", tiles)
    def _(i):
        load_image(i).start()

    barrier = pltpu.get_barrier_semaphore()
    for device in (first, second):
        pl.semaphore_signal(barrier, inc=1, device_id=(device,), device_id_type=MESH)

    scale = jnp.exp(jnp.full((1, 1), scale_ref[0], jnp.float32))
    offset = offset_ref[0]

    def normalize_text(c):
        at = rows_at(c, chunk)
        load_text(c).wait()
        wide = txt_raw[at, :].astype(jnp.float32)
        inverse = inverse_norm(wide)
        txt_inv[at, :] = inverse
        txt_unit[at, :] = (wide * inverse).astype(jnp.bfloat16)

    normalize_text(0)
    pl.semaphore_wait(barrier, 2)

    @phase("unit_text", chunks)
    def _(c):
        if not relayed:
            send_text(0, c, txt_unit, first).start()
            send_text(1, c, txt_unit, second).start()
        else:

            @pl.when(c < AHEAD)
            def _():
                send_text(1, c, txt_unit, second).start()

        @pl.when(c + 1 < chunks)
        def _():
            normalize_text(c + 1)

    @phase("unit_image", tiles)
    def _(i):
        at = rows_at(i, TILE)
        load_image(i).wait()
        wide = img_raw[at, :].astype(jnp.float32)
        inverse = inverse_norm(wide)
        img_inv[at, :] = inverse
        img_unit[at, :] = (wide * inverse).astype(jnp.bfloat16)

    @phase("own_block", tiles)
    def _(i):
        at = rows_at(i, TILE)
        logits = dot_nt(txt_unit[at, :], img_unit[...]) * scale + offset
        slope = 1.0 / (1.0 + jnp.exp(-logits))
        row = lax.broadcasted_iota(jnp.int32, slope.shape, 0) + i * TILE
        column = lax.broadcasted_iota(jnp.int32, slope.shape, 1)
        slope = jnp.where(row == column, slope - 1.0, slope).astype(jnp.bfloat16)
        slopes[0, at, :] = slope
        txt_grad[at, :] = scale * dot_nn(slope, img_unit[...])

    def respond(r, c):
        at = rows_at(c, chunk)
        logits = dot_nt(held[r, at, :], img_unit[...]) * scale + offset
        slope = (1.0 / (1.0 + jnp.exp(-logits))).astype(jnp.bfloat16)
        slopes[r + 1, at, :] = slope
        part[r, at, :] = (scale * dot_nn(slope, img_unit[...])).astype(jnp.bfloat16)

    def finish_image(i):
        at = rows_at(i, TILE)
        grad = dot_tn(slopes[0, :, at], txt_unit[...])
        grad += dot_tn(slopes[1, :, at], held[0])
        grad += dot_tn(slopes[2, :, at], held[1])
        img_out[at, :] = back_norm(img_raw[at, :], img_inv[at, :], scale * grad)

    def finish_text(c):
        at = rows_at(c, chunk)
        grad = txt_grad[at, :]
        send_part(1, c, second).wait_recv()
        grad += returned[1, at, :].astype(jnp.float32)
        if not relayed:
            send_part(0, c, first).wait_recv()
            grad += returned[0, at, :].astype(jnp.float32)
        txt_out[at, :] = back_norm(txt_raw[at, :], txt_inv[at, :], grad)

    if relayed:

        @phase("pass_and_answer", chunks + 1)
        def _(step):
            @pl.when(step < chunks)
            def _():
                send_text(1, step, txt_unit, second).wait_recv()
                send_text(0, step, held.at[1], first).start()

                @pl.when(step + AHEAD < chunks)
                def _():
                    send_text(1, step + AHEAD, txt_unit, second).start()

                @pl.when(step == chunks - 1)
                def _():
                    @pl.loop(0, chunks - 2)
                    def _(c):
                        send_part(0, c, first).start()

                respond(1, step)

            @pl.when(step >= 1)
            def _():
                c = step - 1
                send_text(0, c, held.at[1], first).wait_recv()
                respond(0, c)

                @pl.when(c >= chunks - 2)
                def _():
                    send_part(0, c, first).start()

        @phase("sum_terms", chunks + LAG)
        def _(step):
            @pl.when(step < chunks)
            def _():
                at = rows_at(step, chunk)
                send_part(0, step, first).wait_recv()
                total = part[1, at, :].astype(jnp.float32) + returned[0, at, :].astype(jnp.float32)
                part[1, at, :] = total.astype(jnp.bfloat16)
                send_part(1, step, second).start()

            @pl.when((step % per == 0) & (step // per < tiles))
            def _():
                finish_image(step // per)

            @pl.when(step >= LAG)
            def _():
                finish_text(step - LAG)

    else:

        @phase("answer", chunks)
        def _(c):
            for r, device in ((1, second), (0, first)):
                send_text(r, c, txt_unit, device).wait_recv()
                respond(r, c)
                send_part(r, c, device).start()

        @phase("image_grad", tiles)
        def _(i):
            finish_image(i)

        @phase("text_grad", chunks)
        def _(c):
            finish_text(c)

    @phase("drain", chunks)
    def _(c):
        for r, device in ((0, first), (1, second)):
            send_text(r, c, txt_unit, device).wait_send()
            send_part(r, c, device).wait_send()


def exchange(n, level, img, txt, scale_exponent, additive_offset):
    rows, width = img.shape
    chunk = 64 if 1 << level == n // 4 else 128
    chunks, tiles = rows // chunk, rows // TILE
    block = functools.partial(pltpu.VMEM, (rows, width))
    pair = functools.partial(pltpu.VMEM, (2, rows, width))
    return pl.pallas_call(
        functools.partial(kernel, n, 1 << level, chunk),
        out_shape=(
            jax.ShapeDtypeStruct((rows, width), jnp.bfloat16),
            jax.ShapeDtypeStruct((rows, width), jnp.bfloat16),
        ),
        in_specs=[pl.BlockSpec(memory_space=pltpu.SMEM)] * 2
        + [pl.BlockSpec(memory_space=pl.ANY)] * 2,
        out_specs=[pl.BlockSpec(memory_space=pltpu.VMEM)] * 2,
        scratch_shapes=[
            block(jnp.bfloat16),
            block(jnp.bfloat16),
            block(jnp.bfloat16),
            block(jnp.bfloat16),
            pltpu.VMEM((rows, 1), jnp.float32),
            pltpu.VMEM((rows, 1), jnp.float32),
            pair(jnp.bfloat16),
            pltpu.VMEM((3, rows, rows), jnp.bfloat16),
            block(jnp.float32),
            pair(jnp.bfloat16),
            pair(jnp.bfloat16),
            pltpu.SemaphoreType.DMA((tiles,)),
            pltpu.SemaphoreType.DMA((chunks,)),
            pltpu.SemaphoreType.DMA((2, chunks)),
            pltpu.SemaphoreType.DMA((2, chunks)),
            pltpu.SemaphoreType.DMA((2, chunks)),
            pltpu.SemaphoreType.DMA((2, chunks)),
        ],
        compiler_params=pltpu.CompilerParams(
            collective_id=level, has_side_effects=True, vmem_limit_bytes=40 * 2**20
        ),
        name=f"exchange_{level}",
    )(scale_exponent, additive_offset, img, txt)


def put_kernel(img, txt, img_out, txt_out, sems):
    parts = sems.shape[1]
    size = img.shape[0] // parts
    copies = []
    for p in range(parts):
        at = pl.ds(p * size, size)
        for k, (source, target) in enumerate(((img, img_out), (txt, txt_out))):
            copy = pltpu.make_async_copy(source.at[at], target.at[at], sems.at[k, p])
            copy.start()
            copies.append(copy)
    for copy in copies:
        copy.wait()


def put(img, txt):
    whole = jax.ShapeDtypeStruct(img.shape, img.dtype)
    return pl.pallas_call(
        put_kernel,
        out_shape=(whole, whole),
        in_specs=[pl.BlockSpec(memory_space=pl.ANY)] * 2,
        out_specs=[pl.BlockSpec(memory_space=pltpu.HBM)] * 2,
        scratch_shapes=[pltpu.SemaphoreType.DMA((2, 4))],
        compiler_params=pltpu.CompilerParams(vmem_limit_bytes=16 * 2**20),
        name="put",
    )(img, txt)


def solution(mesh):
    n = mesh.shape["dp"]
    levels = n.bit_length() - 2

    def step(img, txt, scale_exponent, additive_offset, shifts):
        level = 31 - lax.clz(shifts[1])
        branches = [functools.partial(exchange, n, k) for k in range(levels)]
        return put(*lax.switch(level, branches, img, txt, scale_exponent, additive_offset))

    placed = (P("dp", None), P("dp", None), P(), P(), P())
    return jax.shard_map(
        step,
        mesh=mesh,
        in_specs=placed,
        out_specs=(P("dp", None), P("dp", None)),
        check_vma=False,
    )
```

time: 78.2 us -> 141 us (1.80)
  Pallas kernels: 72.1 us -> 137 us
  local copies, waits for them, and re-layouts: 3.46 us -> 1.24 us
    pallas_call x1 -> x2, Pallas kernels: 72.1 us -> 137 us  [the longest x1 136 us: exchange(): pl.pallas_call(functools.partial(kernel, n, 1 << level, chunk), out_shape...]
    unnamed x2 -> x0, local copies, waits for them, and re-layouts: 2.22 us -> none
where the time goes in v2:
time: 141 us
  Pallas kernels  137 us (97%)
  between operations  1.51 us (1%)
    pallas_call x1, Pallas kernels, exchange(): pl.pallas_call(functools.partial(kernel, n, 1 << level, chunk), out_shape...  136 us

profile of v2, /device:TPU:2, one launch (start us, length us, event | category | flops | bytes accessed | tf_op | source)
XLA Modules:
  0.0 140.5 jit_solution(13023551791044049581)
XLA Ops:
  0.6 1.2 slice.3
  2.5 136.1 %conditional.1 = ((bf16[640,1152]{1,0:T(8,128)(2,1)S(1)}, bf16[640,1152]{1,0:T(8,128)(2,1)S(1)})) conditional(s32[]{:T(128)} %bitcast, (f32[1]{0:T(128)}, f32[1]{0:T(128)}, bf16[640,1152]{1,0:T(8,128)(2,1)}, bf16[640,1152]{1,0:T(8,128)(2,1)}) %tuple.28, (f32[1]{0:T(128)}, f32[1]{0:T(128)}, ...), branch_computations={%region_0.0_spmd, %region_1.0_spmd, %region_2.0_spmd, %region_3.0_... | conditional | bytes 8 | solution.py:351
  2.8 135.6 %exchange_4.1 = (bf16[640,1152]{1,0:T(8,128)(2,1)S(1)}, bf16[640,1152]{1,0:T(8,128)(2,1)S(1)}) custom-call(f32[1]{0:T(128)} %get-tuple-element.72.scale_ref, f32[1]{0:T(128)} %get-tuple-element.73.offset_ref, bf16[640,1152]{1,0:T(8,128)(2,1)} %get-tuple-element.74.img_in, bf16[640,1152]{1,0:T(8,128)(2,1)} %get-tuple-element.75.txt_in), custom_call_target="tpu_custom_call" | custom-call | tf_op jit(solution)/shard_map/cond/branch_4_fun/exchange_4/pallas_call | solution.py:282
  138.7 1.7 %put.1 = (bf16[640,1152]{1,0:T(8,128)(2,1)}, bf16[640,1152]{1,0:T(8,128)(2,1)}) custom-call(bf16[640,1152]{1,0:T(8,128)(2,1)S(1)} %get-tuple-element.88.img, bf16[640,1152]{1,0:T(8,128)(2,1)S(1)} %get-tuple-element.89.txt), custom_call_target="tpu_custom_call" | custom-call | tf_op jit(solution)/shard_map/put/pallas_call | solution.py:333

commit v3 on v2

--- a/solution.py
+++ b/solution.py
@@ -9,8 +9,10 @@
 
 MESH = pl.DeviceIdType.MESH
 TILE = 128
-AHEAD = 2
-LAG = 2
+AHEAD = 4
+LAG_TEXT = 6
+EARLY = 3
+LAG = 4
 
 
 def rows_at(index, size):
@@ -51,6 +53,7 @@
     n,
     shift,
     chunk,
+    piece,
     scale_ref,
     offset_ref,
     img_in,
@@ -76,8 +79,8 @@
     part_recv,
 ):
     rows = img_in.shape[0]
-    chunks, tiles = rows // chunk, rows // TILE
-    per = chunks // tiles
+    chunks, pieces, tiles = rows // chunk, rows // piece, rows // TILE
+    per = chunk // piece
     me = lax.axis_index("dp")
     across = me ^ (n // 2)
     near = me ^ shift
@@ -86,7 +89,7 @@
     first, second = (far, near) if relayed else (across, near)
 
     def load_text(c):
-        at = rows_at(c, chunk)
+        at = rows_at(c, piece)
         return pltpu.make_async_copy(txt_in.at[at], txt_raw.at[at], txt_load.at[c])
 
     def load_image(i):
@@ -94,7 +97,7 @@
         return pltpu.make_async_copy(img_in.at[at], img_raw.at[at], img_load.at[i])
 
     def send_text(r, c, source, device):
-        at = rows_at(c, chunk)
+        at = rows_at(c, piece)
         return pltpu.make_async_remote_copy(
             src_ref=source.at[at],
             dst_ref=held.at[r, at],
@@ -105,7 +108,7 @@
         )
 
     def send_part(r, c, device):
-        at = rows_at(c, chunk)
+        at = rows_at(c, piece)
         return pltpu.make_async_remote_copy(
             src_ref=part.at[r, at],
             dst_ref=returned.at[r, at],
@@ -115,7 +118,7 @@
             device_id_type=MESH,
         )
 
-    @phase("load_text", chunks)
+    @phase("load_text", pieces)
     def _(c):
         load_text(c).start()
 
@@ -131,7 +134,7 @@
     offset = offset_ref[0]
 
     def normalize_text(c):
-        at = rows_at(c, chunk)
+        at = rows_at(c, piece)
         load_text(c).wait()
         wide = txt_raw[at, :].astype(jnp.float32)
         inverse = inverse_norm(wide)
@@ -141,7 +144,7 @@
     normalize_text(0)
     pl.semaphore_wait(barrier, 2)
 
-    @phase("unit_text", chunks)
+    @phase("unit_text", pieces)
     def _(c):
         if not relayed:
             send_text(0, c, txt_unit, first).start()
@@ -152,7 +155,7 @@
             def _():
                 send_text(1, c, txt_unit, second).start()
 
-        @pl.when(c + 1 < chunks)
+        @pl.when(c + 1 < pieces)
         def _():
             normalize_text(c + 1)
 
@@ -165,8 +168,7 @@
         img_inv[at, :] = inverse
         img_unit[at, :] = (wide * inverse).astype(jnp.bfloat16)
 
-    @phase("own_block", tiles)
-    def _(i):
+    def own_tile(i):
         at = rows_at(i, TILE)
         logits = dot_nt(txt_unit[at, :], img_unit[...]) * scale + offset
         slope = 1.0 / (1.0 + jnp.exp(-logits))
@@ -191,7 +193,7 @@
         img_out[at, :] = back_norm(img_raw[at, :], img_inv[at, :], scale * grad)
 
     def finish_text(c):
-        at = rows_at(c, chunk)
+        at = rows_at(c, piece)
         grad = txt_grad[at, :]
         send_part(1, c, second).wait_recv()
         grad += returned[1, at, :].astype(jnp.float32)
@@ -202,40 +204,51 @@
 
     if relayed:
 
-        @phase("pass_and_answer", chunks + 1)
+        @phase("pass_and_answer", pieces + LAG_TEXT)
         def _(step):
-            @pl.when(step < chunks)
+            @pl.when(step < pieces)
             def _():
                 send_text(1, step, txt_unit, second).wait_recv()
                 send_text(0, step, held.at[1], first).start()
 
-                @pl.when(step + AHEAD < chunks)
+                @pl.when(step + AHEAD < pieces)
                 def _():
                     send_text(1, step + AHEAD, txt_unit, second).start()
 
-                @pl.when(step == chunks - 1)
+                @pl.when(step % per == per - 2)
                 def _():
-                    @pl.loop(0, chunks - 2)
-                    def _(c):
-                        send_part(0, c, first).start()
-
-                respond(1, step)
-
-            @pl.when(step >= 1)
-            def _():
-                c = step - 1
-                send_text(0, c, held.at[1], first).wait_recv()
-                respond(0, c)
-
-                @pl.when(c >= chunks - 2)
+                    own_tile(step // per)
+
+                @pl.when(step % per == per - 1)
                 def _():
-                    send_part(0, c, first).start()
-
-        @phase("sum_terms", chunks + LAG)
+                    respond(1, step // per)
+
+            @pl.when(step >= LAG_TEXT)
+            def _():
+                p = step - LAG_TEXT
+                send_text(0, p, held.at[1], first).wait_recv()
+
+                @pl.when(p % per == per - 1)
+                def _():
+                    respond(0, p // per)
+
+            @pl.when(step == pieces - 1)
+            def _():
+                @pl.loop(0, EARLY * per)
+                def _(p):
+                    send_part(0, p, first).start()
+
+            @pl.when((step >= EARLY * per + LAG_TEXT) & ((step - LAG_TEXT) % per == per - 1))
+            def _():
+                @pl.loop(0, per)
+                def _(k):
+                    send_part(0, (step - LAG_TEXT) // per * per + k, first).start()
+
+        @phase("sum_terms", pieces + LAG)
         def _(step):
-            @pl.when(step < chunks)
-            def _():
-                at = rows_at(step, chunk)
+            @pl.when(step < pieces)
+            def _():
+                at = rows_at(step, piece)
                 send_part(0, step, first).wait_recv()
                 total = part[1, at, :].astype(jnp.float32) + returned[0, at, :].astype(jnp.float32)
                 part[1, at, :] = total.astype(jnp.bfloat16)
@@ -251,22 +264,28 @@
 
     else:
 
+        @phase("own_block", tiles)
+        def _(i):
+            own_tile(i)
+
         @phase("answer", chunks)
         def _(c):
             for r, device in ((1, second), (0, first)):
-                send_text(r, c, txt_unit, device).wait_recv()
+                for k in range(per):
+                    send_text(r, c * per + k, txt_unit, device).wait_recv()
                 respond(r, c)
-                send_part(r, c, device).start()
+                for k in range(per):
+                    send_part(r, c * per + k, device).start()
 
         @phase("image_grad", tiles)
         def _(i):
             finish_image(i)
 
-        @phase("text_grad", chunks)
+        @phase("text_grad", pieces)
         def _(c):
             finish_text(c)
 
-    @phase("drain", chunks)
+    @phase("drain", pieces)
     def _(c):
         for r, device in ((0, first), (1, second)):
             send_text(r, c, txt_unit, device).wait_send()
@@ -275,12 +294,13 @@
 
 def exchange(n, level, img, txt, scale_exponent, additive_offset):
     rows, width = img.shape
-    chunk = 64 if 1 << level == n // 4 else 128
-    chunks, tiles = rows // chunk, rows // TILE
+    chunk = 128
+    piece = 32 if 1 << level == n // 4 else chunk
+    pieces, tiles = rows // piece, rows // TILE
     block = functools.partial(pltpu.VMEM, (rows, width))
     pair = functools.partial(pltpu.VMEM, (2, rows, width))
     return pl.pallas_call(
-        functools.partial(kernel, n, 1 << level, chunk),
+        functools.partial(kernel, n, 1 << level, chunk, piece),
         out_shape=(
             jax.ShapeDtypeStruct((rows, width), jnp.bfloat16),
             jax.ShapeDtypeStruct((rows, width), jnp.bfloat16),
@@ -301,11 +321,11 @@
             pair(jnp.bfloat16),
             pair(jnp.bfloat16),
             pltpu.SemaphoreType.DMA((tiles,)),
-            pltpu.SemaphoreType.DMA((chunks,)),
-            pltpu.SemaphoreType.DMA((2, chunks)),
-            pltpu.SemaphoreType.DMA((2, chunks)),
-            pltpu.SemaphoreType.DMA((2, chunks)),
-            pltpu.SemaphoreType.DMA((2, chunks)),
+            pltpu.SemaphoreType.DMA((pieces,)),
+            pltpu.SemaphoreType.DMA((2, pieces)),
+            pltpu.SemaphoreType.DMA((2, pieces)),
+            pltpu.SemaphoreType.DMA((2, pieces)),
+            pltpu.SemaphoreType.DMA((2, pieces)),
         ],
         compiler_params=pltpu.CompilerParams(
             collective_id=level, has_side_effects=True, vmem_limit_bytes=40 * 2**20

time: 141 us -> 76.1 us (0.54)
  Pallas kernels: 137 us -> 72.7 us
    pallas_call x1, Pallas kernels: 136 us -> 71 us  [exchange(): pl.pallas_call(functools.partial(kernel, n, 1 << level, chunk, piece), ou...]
where the time goes in v3:
time: 76.1 us; the launch traced here: 76 us
  Pallas kernels  72.7 us (96%)
  between operations  1.51 us (2%)
  local copies, waits for them, and re-layouts  1.24 us (2%)
    pallas_call x1, Pallas kernels, exchange(): pl.pallas_call(functools.partial(kernel, n, 1 << level, chunk, piece), ou...  71 us
    pallas_call x1, Pallas kernels, put(): pl.pallas_call(put_kernel, out_shape=(whole, whole), in_specs=[pl.BlockSp...  1.66 us

profile of v3, /device:TPU:2, one launch (start us, length us, event | category | flops | bytes accessed | tf_op | source)
XLA Modules:
  0.0 76.0 jit_solution(2156752654179676018)
XLA Ops:
  0.6 1.2 %slice.3 = s32[1]{0:T(128)} slice(s32[2]{0:T(128)} %param.16), slice={[1:2]} | slice | bytes 8 | tf_op jit(solution)/shard_map/slice | solution.py:369
  2.5 71.6 %conditional.1 = ((bf16[640,1152]{1,0:T(8,128)(2,1)S(1)}, bf16[640,1152]{1,0:T(8,128)(2,1)S(1)})) conditional(s32[]{:T(128)} %bitcast, (f32[1]{0:T(128)}, f32[1]{0:T(128)}, bf16[640,1152]{1,0:T(8,128)(2,1)}, bf16[640,1152]{1,0:T(8,128)(2,1)}) %tuple.28, (f32[1]{0:T(128)}, f32[1]{0:T(128)}, ...), branch_computations={%region_0.0_spmd, %region_1.0_spmd, %region_2.0_spmd, %region_3.0_... | conditional | bytes 8 | solution.py:371
  2.8 71.0 %exchange_3.1 = (bf16[640,1152]{1,0:T(8,128)(2,1)S(1)}, bf16[640,1152]{1,0:T(8,128)(2,1)S(1)}) custom-call(f32[1]{0:T(128)} %get-tuple-element.68.scale_ref, f32[1]{0:T(128)} %get-tuple-element.69.offset_ref, bf16[640,1152]{1,0:T(8,128)(2,1)} %get-tuple-element.70.img_in, bf16[640,1152]{1,0:T(8,128)(2,1)} %get-tuple-element.71.txt_in), custom_call_target="tpu_custom_call" | custom-call | tf_op jit(solution)/shard_map/cond/branch_3_fun/exchange_3/pallas_call | solution.py:302
  74.1 1.7 %put.1 = (bf16[640,1152]{1,0:T(8,128)(2,1)}, bf16[640,1152]{1,0:T(8,128)(2,1)}) custom-call(bf16[640,1152]{1,0:T(8,128)(2,1)S(1)} %get-tuple-element.88.img, bf16[640,1152]{1,0:T(8,128)(2,1)S(1)} %get-tuple-element.89.txt), custom_call_target="tpu_custom_call" | custom-call | tf_op jit(solution)/shard_map/put/pallas_call | solution.py:353

commit v4 on v3

--- a/solution.py
+++ b/solution.py
@@ -54,6 +54,7 @@
     shift,
     chunk,
     piece,
+    text_piece,
     scale_ref,
     offset_ref,
     img_in,
@@ -81,6 +82,7 @@
     rows = img_in.shape[0]
     chunks, pieces, tiles = rows // chunk, rows // piece, rows // TILE
     per = chunk // piece
+    text_pieces = rows // text_piece
     me = lax.axis_index("dp")
     across = me ^ (n // 2)
     near = me ^ shift
@@ -89,7 +91,7 @@
     first, second = (far, near) if relayed else (across, near)
 
     def load_text(c):
-        at = rows_at(c, piece)
+        at = rows_at(c, text_piece)
         return pltpu.make_async_copy(txt_in.at[at], txt_raw.at[at], txt_load.at[c])
 
     def load_image(i):
@@ -97,7 +99,7 @@
         return pltpu.make_async_copy(img_in.at[at], img_raw.at[at], img_load.at[i])
 
     def send_text(r, c, source, device):
-        at = rows_at(c, piece)
+        at = rows_at(c, text_piece)
         return pltpu.make_async_remote_copy(
             src_ref=source.at[at],
             dst_ref=held.at[r, at],
@@ -118,7 +120,11 @@
             device_id_type=MESH,
         )
 
-    @phase("load_text", pieces)
+    barrier = pltpu.get_barrier_semaphore()
+    for device in (first, second):
+        pl.semaphore_signal(barrier, inc=1, device_id=(device,), device_id_type=MESH)
+
+    @phase("load_text", text_pieces)
     def _(c):
         load_text(c).start()
 
@@ -126,15 +132,11 @@
     def _(i):
         load_image(i).start()
 
-    barrier = pltpu.get_barrier_semaphore()
-    for device in (first, second):
-        pl.semaphore_signal(barrier, inc=1, device_id=(device,), device_id_type=MESH)
-
     scale = jnp.exp(jnp.full((1, 1), scale_ref[0], jnp.float32))
     offset = offset_ref[0]
 
     def normalize_text(c):
-        at = rows_at(c, piece)
+        at = rows_at(c, text_piece)
         load_text(c).wait()
         wide = txt_raw[at, :].astype(jnp.float32)
         inverse = inverse_norm(wide)
@@ -144,7 +146,7 @@
     normalize_text(0)
     pl.semaphore_wait(barrier, 2)
 
-    @phase("unit_text", pieces)
+    @phase("unit_text", text_pieces)
     def _(c):
         if not relayed:
             send_text(0, c, txt_unit, first).start()
@@ -155,7 +157,7 @@
             def _():
                 send_text(1, c, txt_unit, second).start()
 
-        @pl.when(c + 1 < pieces)
+        @pl.when(c + 1 < text_pieces)
         def _():
             normalize_text(c + 1)
 
@@ -268,14 +270,17 @@
         def _(i):
             own_tile(i)
 
-        @phase("answer", chunks)
-        def _(c):
+        @phase("answer", text_pieces)
+        def _(t):
             for r, device in ((1, second), (0, first)):
-                for k in range(per):
-                    send_text(r, c * per + k, txt_unit, device).wait_recv()
-                respond(r, c)
-                for k in range(per):
-                    send_part(r, c * per + k, device).start()
+                send_text(r, t, txt_unit, device).wait_recv()
+
+            @pl.loop(0, text_piece // chunk)
+            def _(k):
+                c = t * (text_piece // chunk) + k
+                for r, device in ((1, second), (0, first)):
+                    respond(r, c)
+                    send_part(r, c, device).start()
 
         @phase("image_grad", tiles)
         def _(i):
@@ -288,19 +293,25 @@
     @phase("drain", pieces)
     def _(c):
         for r, device in ((0, first), (1, second)):
+            send_part(r, c, device).wait_send()
+
+    @phase("drain_text", text_pieces)
+    def _(c):
+        for r, device in ((0, first), (1, second)):
             send_text(r, c, txt_unit, device).wait_send()
-            send_part(r, c, device).wait_send()
 
 
 def exchange(n, level, img, txt, scale_exponent, additive_offset):
     rows, width = img.shape
-    chunk = 128
-    piece = 32 if 1 << level == n // 4 else chunk
-    pieces, tiles = rows // piece, rows // TILE
+    if 1 << level == n // 4:
+        chunk, piece, text_piece = 128, 32, 32
+    else:
+        chunk, piece, text_piece = 160, 160, 160
+    pieces, text_pieces, tiles = rows // piece, rows // text_piece, rows // TILE
     block = functools.partial(pltpu.VMEM, (rows, width))
     pair = functools.partial(pltpu.VMEM, (2, rows, width))
     return pl.pallas_call(
-        functools.partial(kernel, n, 1 << level, chunk, piece),
+        functools.partial(kernel, n, 1 << level, chunk, piece, text_piece),
         out_shape=(
             jax.ShapeDtypeStruct((rows, width), jnp.bfloat16),
             jax.ShapeDtypeStruct((rows, width), jnp.bfloat16),
@@ -321,9 +332,9 @@
             pair(jnp.bfloat16),
             pair(jnp.bfloat16),
             pltpu.SemaphoreType.DMA((tiles,)),
-            pltpu.SemaphoreType.DMA((pieces,)),
-            pltpu.SemaphoreType.DMA((2, pieces)),
-            pltpu.SemaphoreType.DMA((2, pieces)),
+            pltpu.SemaphoreType.DMA((text_pieces,)),
+            pltpu.SemaphoreType.DMA((2, text_pieces)),
+            pltpu.SemaphoreType.DMA((2, text_pieces)),
             pltpu.SemaphoreType.DMA((2, pieces)),
             pltpu.SemaphoreType.DMA((2, pieces)),
         ],
@@ -335,15 +346,12 @@
 
 
 def put_kernel(img, txt, img_out, txt_out, sems):
-    parts = sems.shape[1]
-    size = img.shape[0] // parts
-    copies = []
-    for p in range(parts):
-        at = pl.ds(p * size, size)
-        for k, (source, target) in enumerate(((img, img_out), (txt, txt_out))):
-            copy = pltpu.make_async_copy(source.at[at], target.at[at], sems.at[k, p])
-            copy.start()
-            copies.append(copy)
+    copies = [
+        pltpu.make_async_copy(img, img_out, sems.at[0]),
+        pltpu.make_async_copy(txt, txt_out, sems.at[1]),
+    ]
+    for copy in copies:
+        copy.start()
     for copy in copies:
         copy.wait()
 
@@ -355,7 +363,7 @@
         out_shape=(whole, whole),
         in_specs=[pl.BlockSpec(memory_space=pl.ANY)] * 2,
         out_specs=[pl.BlockSpec(memory_space=pltpu.HBM)] * 2,
-        scratch_shapes=[pltpu.SemaphoreType.DMA((2, 4))],
+        scratch_shapes=[pltpu.SemaphoreType.DMA((2,))],
         compiler_params=pltpu.CompilerParams(vmem_limit_bytes=16 * 2**20),
         name="put",
     )(img, txt)

time: 76.1 us -> 76 us (level)
  no operation moved by 1% of the time
where the time goes in v4:
time: 76 us; the launch traced here: 75.9 us
  Pallas kernels  72.6 us (96%)
  between operations  1.51 us (2%)
  local copies, waits for them, and re-layouts  1.24 us (2%)
    pallas_call x1, Pallas kernels, exchange(): pl.pallas_call(functools.partial(kernel, n, 1 << level, chunk, piece, tex...  71 us
    pallas_call x1, Pallas kernels, put(): pl.pallas_call(put_kernel, out_shape=(whole, whole), in_specs=[pl.BlockSp...  1.61 us

profile of v4, /device:TPU:2, one launch (start us, length us, event | category | flops | bytes accessed | tf_op | source)
XLA Modules:
  0.0 75.9 jit_solution(17173954217679933801)
XLA Ops:
  0.6 1.2 %slice.3 = s32[1]{0:T(128)} slice(s32[2]{0:T(128)} %param.16), slice={[1:2]} | slice | bytes 8 | tf_op jit(solution)/shard_map/slice | solution.py:377
  2.5 71.5 %conditional.1 = ((bf16[640,1152]{1,0:T(8,128)(2,1)S(1)}, bf16[640,1152]{1,0:T(8,128)(2,1)S(1)})) conditional(s32[]{:T(128)} %bitcast, (f32[1]{0:T(128)}, f32[1]{0:T(128)}, bf16[640,1152]{1,0:T(8,128)(2,1)}, bf16[640,1152]{1,0:T(8,128)(2,1)}) %tuple.28, (f32[1]{0:T(128)}, f32[1]{0:T(128)}, ...), branch_computations={%region_0.0_spmd, %region_1.0_spmd, %region_2.0_spmd, %region_3.0_... | conditional | bytes 8 | solution.py:379
  2.8 71.0 %exchange_3.1 = (bf16[640,1152]{1,0:T(8,128)(2,1)S(1)}, bf16[640,1152]{1,0:T(8,128)(2,1)S(1)}) custom-call(f32[1]{0:T(128)} %get-tuple-element.68.scale_ref, f32[1]{0:T(128)} %get-tuple-element.69.offset_ref, bf16[640,1152]{1,0:T(8,128)(2,1)} %get-tuple-element.70.img_in, bf16[640,1152]{1,0:T(8,128)(2,1)} %get-tuple-element.71.txt_in), custom_call_target="tpu_custom_call" | custom-call | tf_op jit(solution)/shard_map/cond/branch_3_fun/exchange_3/pallas_call | solution.py:313
  74.1 1.6 %put.1 = (bf16[640,1152]{1,0:T(8,128)(2,1)}, bf16[640,1152]{1,0:T(8,128)(2,1)}) custom-call(bf16[640,1152]{1,0:T(8,128)(2,1)S(1)} %get-tuple-element.88.img, bf16[640,1152]{1,0:T(8,128)(2,1)S(1)} %get-tuple-element.89.txt), custom_call_target="tpu_custom_call" | custom-call | tf_op jit(solution)/shard_map/put/pallas_call | solution.py:361

commit v5 on v4

--- a/solution.py
+++ b/solution.py
@@ -9,6 +9,7 @@
 
 MESH = pl.DeviceIdType.MESH
 TILE = 128
+STRIP = 32
 AHEAD = 4
 LAG_TEXT = 6
 EARLY = 3
@@ -135,13 +136,18 @@
     scale = jnp.exp(jnp.full((1, 1), scale_ref[0], jnp.float32))
     offset = offset_ref[0]
 
+    def normalize(raw, inverses, units, begin, count):
+        @pl.loop(begin, begin + count)
+        def _(k):
+            at = rows_at(k, STRIP)
+            wide = raw[at, :].astype(jnp.float32)
+            inverse = inverse_norm(wide)
+            inverses[at, :] = inverse
+            units[at, :] = (wide * inverse).astype(jnp.bfloat16)
+
     def normalize_text(c):
-        at = rows_at(c, text_piece)
         load_text(c).wait()
-        wide = txt_raw[at, :].astype(jnp.float32)
-        inverse = inverse_norm(wide)
-        txt_inv[at, :] = inverse
-        txt_unit[at, :] = (wide * inverse).astype(jnp.bfloat16)
+        normalize(txt_raw, txt_inv, txt_unit, c * (text_piece // STRIP), text_piece // STRIP)
 
     normalize_text(0)
     pl.semaphore_wait(barrier, 2)
@@ -163,12 +169,8 @@
 
     @phase("unit_image", tiles)
     def _(i):
-        at = rows_at(i, TILE)
         load_image(i).wait()
-        wide = img_raw[at, :].astype(jnp.float32)
-        inverse = inverse_norm(wide)
-        img_inv[at, :] = inverse
-        img_unit[at, :] = (wide * inverse).astype(jnp.bfloat16)
+        normalize(img_raw, img_inv, img_unit, i * (TILE // STRIP), TILE // STRIP)
 
     def own_tile(i):
         at = rows_at(i, TILE)
@@ -278,9 +280,10 @@
             @pl.loop(0, text_piece // chunk)
             def _(k):
                 c = t * (text_piece // chunk) + k
-                for r, device in ((1, second), (0, first)):
-                    respond(r, c)
-                    send_part(r, c, device).start()
+                @pl.loop(0, 2)
+                def _(j):
+                    respond(1 - j, c)
+                    send_part(1 - j, c, jnp.where(j == 0, second, first)).start()
 
         @phase("image_grad", tiles)
         def _(i):

time: 76 us -> 76.2 us (level)
  no operation moved by 1% of the time
where the time goes in v5:
time: 76.2 us; the launch traced here: 75.4 us
  Pallas kernels  72.4 us (95%)
  between operations  1.47 us (2%)
  local copies, waits for them, and re-layouts  1.24 us (2%)
    pallas_call x1, Pallas kernels, exchange(): pl.pallas_call(functools.partial(kernel, n, 1 << level, chunk, piece, tex...  70.8 us
    pallas_call x1, Pallas kernels, put(): pl.pallas_call(put_kernel, out_shape=(whole, whole), in_specs=[pl.BlockSp...  1.61 us

profile of v5, /device:TPU:2, one launch (start us, length us, event | category | flops | bytes accessed | tf_op | source)
XLA Modules:
  0.0 75.4 jit_solution(2398128958833327467)
XLA Ops:
  0.6 1.2 %slice.3 = s32[1]{0:T(128)} slice(s32[2]{0:T(128)} %param.16), slice={[1:2]} | slice | bytes 8 | tf_op jit(solution)/shard_map/slice | solution.py:380
  2.5 71.1 %conditional.1 = ((bf16[640,1152]{1,0:T(8,128)(2,1)S(1)}, bf16[640,1152]{1,0:T(8,128)(2,1)S(1)})) conditional(s32[]{:T(128)} %bitcast, (f32[1]{0:T(128)}, f32[1]{0:T(128)}, bf16[640,1152]{1,0:T(8,128)(2,1)}, bf16[640,1152]{1,0:T(8,128)(2,1)}) %tuple.28, (f32[1]{0:T(128)}, f32[1]{0:T(128)}, ...), branch_computations={%region_0.0_spmd, %region_1.0_spmd, %region_2.0_spmd, %region_3.0_... | conditional | bytes 8 | solution.py:382
  2.5 70.8 %exchange_1.1 = (bf16[640,1152]{1,0:T(8,128)(2,1)S(1)}, bf16[640,1152]{1,0:T(8,128)(2,1)S(1)}) custom-call(f32[1]{0:T(128)} %get-tuple-element.60.scale_ref, f32[1]{0:T(128)} %get-tuple-element.61.offset_ref, bf16[640,1152]{1,0:T(8,128)(2,1)} %get-tuple-element.62.img_in, bf16[640,1152]{1,0:T(8,128)(2,1)} %get-tuple-element.63.txt_in), custom_call_target="tpu_custom_call" | custom-call | tf_op jit(solution)/shard_map/cond/branch_1_fun/exchange_1/pallas_call | solution.py:316
  73.6 1.6 %put.1 = (bf16[640,1152]{1,0:T(8,128)(2,1)}, bf16[640,1152]{1,0:T(8,128)(2,1)}) custom-call(bf16[640,1152]{1,0:T(8,128)(2,1)S(1)} %get-tuple-element.88.img, bf16[640,1152]{1,0:T(8,128)(2,1)S(1)} %get-tuple-element.89.txt), custom_call_target="tpu_custom_call" | custom-call | tf_op jit(solution)/shard_map/put/pallas_call | solution.py:364
